TPU v7x, 256 devices: a whole 4x4x8 slice. The times are simulated.
256 devices in a mesh: row: 16 (over y, z_lo), col: 16 (over x, z_hi, core).
Axes of the slice: x: 4, y: 4, z: 8 (z_hi: 2, z_lo: 4; z = z_hi * 4 + z_lo), core: 2. Of those that a mesh axis runs over, the one named last changes fastest.
Arguments:
- activations: bfloat16 [2048, 28672], P('col', 'row'), may hold values from -36 to 36
- output_gradient: bfloat16 [2048, 8192], P('row', 'col'), may hold values from -6 to 6
- frozen_weight: bfloat16 [28672, 8192], P('row', 'col'), may hold values from -0.0390625 to 0.0390625
- sparsity_mask_pattern: int32 [7168, 8192], P('row', 'col'), may hold values from 0 to 5
- adapter_left_factor: bfloat16 [28672, 16], P('row'), may hold values from -0.19921875 to 0.19921875
- adapter_right_factor: bfloat16 [16, 8192], P(None, 'col'), may hold values from -0.359375 to 0.359375
Outputs:
- input_grad: bfloat16 [2048, 28672], P('col', 'row')
- left_grad: float32 [28672, 16], P('row')
- right_grad: float32 [16, 8192], P(None, 'col')
Inputs may be any that keep to these rules, and one draw needn't show every extreme that they name: `sparsity_mask_pattern`: a pattern number of the 2:4 mask.
All inputs are finite; a program needn't handle non-finite values.
Results may differ from a plain program's by a relative error of at most 0.005.
Values may be sent and summed in bfloat16 or wider, within the bound.
A program may use at most 64 MiB of HBM per device.

v0:
```python
import jax
import jax.numpy as jnp
from jax import lax
from jax.sharding import PartitionSpec as P

PAIRS = ((0, 1), (0, 2), (0, 3), (1, 2), (1, 3), (2, 3))
ADAPTER_SCALE = 2.0


def expand_mask(code):
    groups = []
    for column in range(4):
        kept = jnp.zeros(code.shape, jnp.float32)
        for pattern in range(6):
            if column in PAIRS[pattern]:
                kept = kept + (code == pattern).astype(jnp.float32)
        groups.append(kept)
    stacked = jnp.stack(groups, axis=1)
    return stacked.reshape(code.shape[0] * 4, code.shape[1])


def input_sums_of(grad_rows, merged):
    return lax.psum_scatter(
        lax.dot_general(
            grad_rows, merged, (((1,), (1,)), ((), ())), preferred_element_type=jnp.float32
        ),
        "col",
        scatter_dimension=0,
        tiled=True,
    )


def weight_grad_of(activations, grad_rows):
    return lax.dot_general(
        lax.all_gather(activations, "col", axis=0, tiled=True),
        grad_rows,
        (((0,), (0,)), ((), ())),
        preferred_element_type=jnp.float32,
    )


def per_device(
    activations,
    output_gradient,
    frozen_weight,
    sparsity_mask_pattern,
    adapter_left_factor,
    adapter_right_factor,
):
    masked = expand_mask(sparsity_mask_pattern)
    low_rank_update = jnp.dot(
        adapter_left_factor, adapter_right_factor, preferred_element_type=jnp.float32
    )
    merged = (
        masked * (frozen_weight.astype(jnp.float32) + ADAPTER_SCALE * low_rank_update)
    ).astype(jnp.bfloat16)
    grad_rows = lax.all_gather(output_gradient, "row", axis=0, tiled=True)
    all_tokens = grad_rows.shape[0]
    input_sums = input_sums_of(grad_rows, merged)
    held, later_rows = lax.optimization_barrier((input_sums, activations))
    weight_grad = weight_grad_of(later_rows, grad_rows)
    input_grad = held.astype(jnp.bfloat16)
    pruned_gradient = (masked * weight_grad / all_tokens).astype(jnp.bfloat16)
    left_partial = ADAPTER_SCALE * lax.dot_general(
        pruned_gradient,
        adapter_right_factor,
        (((1,), (1,)), ((), ())),
        preferred_element_type=jnp.float32,
    )
    right_partial = ADAPTER_SCALE * lax.dot_general(
        adapter_left_factor,
        pruned_gradient,
        (((0,), (0,)), ((), ())),
        preferred_element_type=jnp.float32,
    )
    right_grad = lax.psum(right_partial, "row")
    left_grad = lax.psum(left_partial, "col")
    return (input_grad, left_grad, right_grad)


def solution(mesh):
    in_specs = (
        P("col", "row"),
        P("row", "col"),
        P("row", "col"),
        P("row", "col"),
        P("row", None),
        P(None, "col"),
    )
    out_specs = (P("col", "row"), P("row", None), P(None, "col"))
    return jax.shard_map(
        per_device, mesh=mesh, in_specs=in_specs, out_specs=out_specs, check_vma=False
    )
```

profile of v0, /device:TPU:1, one launch (start us, length us, event | category | flops | bytes accessed | tf_op | source)
XLA Modules:
  0.0 587.2 jit_solution(565895379995326784)
XLA Ops:
  7.2 0.0 copy-start
  7.2 0.0 copy-start.1
  7.2 0.0 all-gather.3.cloned.1.call-start
  7.2 0.7 all-gather.3.cloned.1.call-update
  7.9 0.0 reduce-scatter.2.cloned.1.call-start
  8.0 1.7 fusion.1
  9.7 1.6 fusion.2
  11.3 0.0 copy-done.1
  11.3 0.3 fusion.3
  11.6 0.2 fusion.4
  11.9 0.4 pad_maximum_fusion
  12.2 4.2 copy.9
  16.4 0.0 copy-start.2
  16.4 0.0 copy-start.3
  16.4 5.2 reshape.9
  21.7 70.0 %all-gather.3.cloned.1.call-done = bf16[2048,512]{1,0:T(8,128)(2,1)} async-done(((bf16[128,512]{1,0:T(8,128)(2,1)}), bf16[2048,512]{1,0:T(8,128)(2,1)}) %all-gather.3.cloned.1.call-update) | async-done | bytes 2097168 | tf_op jit(solution)/shard_map/all_gather | solution.py:57
  91.7 0.0 copy-done
  91.7 0.0 copy-done.2
  91.7 0.0 copy-done.3
  91.7 9.9 %convolution_bitcast_fusion = f32[2048,1792]{0,1:T(8,128)} fusion(bf16[2048,512]{1,0:T(8,128)(2,1)} %all-gather.3.cloned.1.call-done, f32[1792,512]{1,0:T(8,128)} %reshape.9, bf16[1792,512]{1,0:T(8,128)(2,1)S(1)} %copy-done.3, bf16[1792,16]{0,1:T(8,128)(2,1)S(1)} %copy-done, bf16[16,512]{1,0:T(8,128)(2,1)S(1)} %copy-done.2), kind=kOutput, calls=%fused_computation | convolution fusion | flops 3792044032 | bytes 22355968 | tf_op jit(solution)/shard_map/dot_general | solution.py:24
  101.6 0.0 reduce-scatter.2.cloned.1.call-update
  101.6 0.0 all-gather.5.cloned.1.call-start
  101.7 202.2 %reduce-scatter.2.cloned.1.call-done = f32[128,1792]{0,1:T(8,128)} async-done(((f32[2048,1792]{0,1:T(8,128)}), f32[128,1792]{0,1:T(8,128)}) %reduce-scatter.2.cloned.1.call-update) | async-done | bytes 917520 | tf_op jit(solution)/shard_map/reduce_scatter | solution.py:23
  303.9 0.0 all-gather.5.cloned.1.call-update
  303.9 0.0 all-reduce.2.cloned.1.call-start
  303.9 1.2 convert_element_type.44
  305.2 1.0 copy.10
  306.2 97.1 %all-gather.5.cloned.1.call-done = bf16[2048,1792]{1,0:T(8,128)(2,1)} async-done(((bf16[128,1792]{1,0:T(8,128)(2,1)}), bf16[2048,1792]{1,0:T(8,128)(2,1)}) %all-gather.5.cloned.1.call-update) | async-done | bytes 7340048 | tf_op jit(solution)/shard_map/all_gather | solution.py:35
  403.3 8.8 %multiply_convert_fusion = bf16[1792,512]{1,0:T(8,128)(2,1)S(1)} fusion(f32[1792,512]{1,0:T(8,128)} %reshape.9, bf16[2048,1792]{1,0:T(8,128)(2,1)} %all-gather.5.cloned.1.call-done, bf16[2048,512]{1,0:T(8,128)(2,1)} %all-gather.3.cloned.1.call-done), kind=kOutput, calls=%fused_computation.2 | convolution fusion | flops 3760848896 | bytes 14942208 | tf_op jit(solution)/shard_map/dot_general | solution.py:34
  412.1 1.2 convolution_multiply_fusion
  413.3 0.0 all-reduce.2.cloned.1.call-update
  413.3 0.3 fusion
  413.7 64.2 %psum.15 = f32[16,512]{1,0:T(8,128)} all-reduce(f32[16,512]{1,0:T(8,128)S(1)} %fusion), channel_id=1, replica_groups=mesh['row'=16,'col'=16] {'row'}, use_global_device_ids=true, to_apply=%region_2.0 | all-reduce | flops 8192 | bytes 65536 | tf_op jit(solution)/shard_map/psum | solution.py:76
  477.9 101.2 %all-reduce.2.cloned.1.call-done = f32[1792,16]{0,1:T(8,128)} async-done(((f32[1792,16]{0,1:T(8,128)}), f32[1792,16]{0,1:T(8,128)}) %all-reduce.2.cloned.1.call-update) | async-done | bytes 114704 | tf_op jit(solution)/shard_map/psum | solution.py:77
  579.1 1.6 copy.12
Async XLA Ops:
  7.2 84.5 %copy-start = (bf16[1792,16]{0,1:T(8,128)(2,1)S(1)}, bf16[1792,16]{0,1:T(8,128)(2,1)}, u32[]{:S(2)}) copy-start(bf16[1792,16]{0,1:T(8,128)(2,1)} %param.10) | copy-start | bytes 172036
  7.2 4.1 copy-start.1
  7.2 84.5 %all-gather.3.cloned.1.call-start = ((), (), s32[]{:S(2)}) async-start(), calls=%async_computation.1 | async-start | bytes 2228224 | tf_op jit(solution)/shard_map/all_gather | solution.py:57
  7.9 295.9 %reduce-scatter.2.cloned.1.call-start = ((), (), s32[]{:S(2)}) async-start(), calls=%async_computation.2 | async-start | bytes 15597568 | tf_op jit(solution)/shard_map/reduce_scatter | solution.py:23
  16.4 75.3 %copy-start.2 = (bf16[16,512]{1,0:T(8,128)(2,1)S(1)}, bf16[16,512]{1,0:T(8,128)(2,1)}, u32[]{:S(2)}) copy-start(bf16[16,512]{1,0:T(8,128)(2,1)} %param.11) | copy-start | bytes 49156
  16.4 75.3 %copy-start.3 = (bf16[1792,512]{1,0:T(8,128)(2,1)S(1)}, bf16[1792,512]{1,0:T(8,128)(2,1)}, u32[]{:S(2)}) copy-start(bf16[1792,512]{1,0:T(8,128)(2,1)} %param.8) | copy-start | bytes 5505028
  101.6 301.7 %all-gather.5.cloned.1.call-start = ((), (), s32[]{:S(2)}) async-start(), calls=%async_computation.3 | async-start | bytes 7798784 | tf_op jit(solution)/shard_map/all_gather | solution.py:35
  303.9 275.2 %all-reduce.2.cloned.1.call-start = ((), (), s32[]{:S(2)}) async-start(), calls=%async_computation.4 | async-start | bytes 229376 | tf_op jit(solution)/shard_map/psum | solution.py:77
Sparse Core Ops, SparseCore 0:
  9.8 81.8 all-gather.2
  101.8 202.0 reduce-scatter.1
  306.9 96.3 all-gather.4
  413.5 165.5 all-reduce.1
where the time goes:
time: 588 us; the launch traced here: 587 us
  waiting for transfers between devices  471 us (80%)
  blocking collectives  64.2 us (11%)
  matrix products  20.3 us (3%)
  between operations  13.8 us (2%)
  local copies, waits for them, and re-layouts  12 us (2%)
    reduce_scatter x1, waiting for transfers between devices, input_sums_of(): lax.psum_scatter(lax.dot_general(grad_rows, merged, (((1,), (1,)), ((), (...  202 us
    psum x1, waiting for transfers between devices, per_device(): left_grad = lax.psum(left_partial, 'col')  101 us
    all_gather x1, waiting for transfers between devices, weight_grad_of(): lax.all_gather(activations, 'col', axis=0, tiled=True)  97.1 us
    all_gather x1, waiting for transfers between devices, per_device(): grad_rows = lax.all_gather(output_gradient, 'row', axis=0, tiled=True)  70 us
    psum x1, blocking collectives, per_device(): right_grad = lax.psum(right_partial, 'row')  64.2 us
  transfers between devices with their start and end apart: 4, of which 4 were waited for; matrix products, arithmetic and copies ran while one was open for 3% of the time, Pallas kernels for 0%

commit v1 on v0

v1 whole, which is shorter than its diff:
```python
import functools

import jax
import jax.numpy as jnp
from jax import lax
from jax.experimental import pallas as pl
from jax.experimental.pallas import tpu as pltpu
from jax.sharding import PartitionSpec as P

MESH = pl.DeviceIdType.MESH
BF16, F32 = jnp.bfloat16, jnp.float32
TOKENS, RANK = 2048, 16
TOK, HID, COLS = 128, 1792, 512
HALF, BOTH = HID // 2, 2 * COLS
NT = (((1,), (1,)), ((), ()))
TN = (((0,), (0,)), ((), ()))
HT = 128
WIDE = ((0, 256), (256, 256), (512, 256), (768, 128))

NUMBERS = {}


def numbered(name, count):
    NUMBERS[name] = sum(c for _, c in NUMBERS.values()), count


for _name, _count in (
    ("AX", 4), ("AZ", 2), ("AS", 1), ("AF", 2), ("AP", 4), ("APF", 2),
    ("GZ", 3), ("GY", 8), ("GF", 4), ("GS", 16),
    ("W", 1), ("C", 1), ("R", 1),
    ("S1", 4), ("S2", 4), ("S3", 4), ("Z", 1), ("O", 1),
    ("LX", 3), ("LZ", 3), ("RC", 1), ("RY", 3), ("RZ", 3),
):
    numbered(_name, _count)
COPIES = sum(c for _, c in NUMBERS.values())


def number(name, index=0):
    return NUMBERS[name][0] + index


def merge_tiles(slot, w_buf, c_buf, r_buf, l_buf, mask_buf, m_buf):
    cols = pl.ds(slot * COLS, COLS)
    groups = HT // 4
    row = lax.broadcasted_iota(jnp.int32, (HT, HT), 0)
    lane = lax.broadcasted_iota(jnp.int32, (HT, HT), 1)
    hit = (row % 4 == lane // groups) & (row // 4 == lane % groups)
    spread = jnp.where(hit, 1.0, 0.0).astype(BF16)
    right = r_buf[:, cols]

    def tile(i, _):
        code = c_buf[pl.ds(pl.multiple_of(i * groups, groups), groups), cols]
        is0, is1, is2 = code == 0, code == 1, code == 2
        is3, is4, is5 = code == 3, code == 4, code == 5
        kept = (is0 | is1 | is2, is0 | is3 | is4, is1 | is3 | is5, is2 | is4 | is5)
        kept = jnp.concatenate([jnp.where(b, 1.0, 0.0) for b in kept], axis=0).astype(BF16)
        mask = jnp.dot(spread, kept, preferred_element_type=F32)
        rows = pl.ds(pl.multiple_of(i * HT, HT), HT)
        low = jnp.dot(l_buf[rows, :], right, preferred_element_type=F32)
        merged = mask * (w_buf[rows, cols].astype(F32) + 2.0 * low)
        mask_buf[rows, cols] = mask.astype(BF16)
        m_buf[rows, cols] = merged.astype(BF16)
        return 0

    lax.fori_loop(0, HALF // HT, tile, 0)


def product(i, x_dest, g_buf, m_buf, p_buf):
    first = pl.multiple_of(x_dest * 4 * TOK, 4 * TOK)
    for at, size in WIDE:
        p_buf[i, :, at : at + size] = lax.dot_general(
            g_buf[pl.ds(first, 4 * TOK), :], m_buf[at : at + size, :], NT, preferred_element_type=F32
        )


def turn(a_buf, at_buf, first, count):
    def block(i, _):
        toks = pl.ds(pl.multiple_of(i * TOK, TOK), TOK)
        at_buf[:, toks] = a_buf[toks, :].T
        return 0

    lax.fori_loop(first, first + count, block, 0)


def factor_grads(at_buf, g_buf, mask_buf, r_buf, l_buf, left, right):
    left[...] = jnp.zeros_like(left)
    step = 256

    def tile(n, _):
        cols = pl.ds(pl.multiple_of(n * step, step), step)
        total = jnp.zeros((RANK, step), F32)
        for half in range(2):
            rows = pl.ds(half * (HALF // 2), HALF // 2)
            grad = jnp.dot(at_buf[rows, :], g_buf[:, cols], preferred_element_type=F32)
            pruned = (mask_buf[rows, cols].astype(F32) * grad * (1.0 / TOKENS)).astype(BF16)
            total += lax.dot_general(l_buf[rows, :], pruned, TN, preferred_element_type=F32)
            left[half] += 2.0 * lax.dot_general(
                r_buf[:, cols], pruned, NT, preferred_element_type=F32
            )
        right[:, cols] = 2.0 * total
        return 0

    lax.fori_loop(0, BOTH // step, tile, 0)


def kernel(
    a, g, w, code, lf, rf, out, left_out, right_out,
    a_buf, at_buf, g_buf, w_buf, c_buf, r_buf, l_buf, mask_buf, m_buf,
    p_buf, s_buf, got1, got2, z_send, z_got, o_send, o_own,
    lpart, lx, lz, lgot, rpart, rgot, ry, rz,
    send_sem, recv_sem, local_sem,
):
    row, col = lax.axis_index("row"), lax.axis_index("col")
    y, zl = row // 4, row % 4
    x, zh, k = col // 4, (col // 2) % 2, col % 2
    other = 1 - zh

    def device(y_=y, zl_=zl, x_=x, zh_=zh, k_=k):
        return (y_ * 4 + zl_, x_ * 4 + zh_ * 2 + k_)

    def wrap(v):
        return v % 4

    x_at = (wrap(x + 1), wrap(x + 3))
    y_at = (wrap(y + 1), wrap(y + 3))
    sibling = device(k_=1 - k)
    peers = [sibling]
    peers += [device(x_=x_at[d], k_=j) for d in range(2) for j in range(2)]
    peers += [device(x_=wrap(x + 2))]
    peers += [device(zh_=other, k_=j) for j in range(2)]
    peers += [device(y_=wrap(y + i)) for i in range(1, 4)]
    peers += [device(zl_=wrap(zl + i)) for i in range(1, 4)]

    pending = []

    def send(src, dst, n, to, recv_n=None):
        copy = pltpu.make_async_remote_copy(
            src_ref=src, dst_ref=dst, send_sem=send_sem.at[n],
            recv_sem=recv_sem.at[n if recv_n is None else recv_n],
            device_id=to, device_id_type=MESH,
        )
        copy.start()
        pending.append(copy)

    def arrived(dst, n):
        pltpu.make_async_remote_copy(
            src_ref=dst, dst_ref=dst, send_sem=send_sem.at[n], recv_sem=recv_sem.at[n],
            device_id=sibling, device_id_type=MESH,
        ).wait_recv()

    def tokens_of(x_, zh_, k_):
        return pl.ds(pl.multiple_of((x_ * 4 + zh_ * 2 + k_) * TOK, TOK), TOK)

    def a_block(x_, zh_, k_):
        return a_buf.at[tokens_of(x_, zh_, k_), :]

    def g_block(y_, zl_, slot=0):
        return g_buf.at[pl.ds(pl.multiple_of((y_ * 4 + zl_) * TOK, TOK), TOK), pl.ds(slot * COLS, COLS)]

    def half(j):
        return pl.ds(pl.multiple_of(j * HALF, HALF), HALF)

    def quarter(j):
        return pl.ds(pl.multiple_of(j * (HALF // 4), HALF // 4), HALF // 4)

    own_cols, sib_cols = pl.ds(0, COLS), pl.ds(COLS, COLS)

    locals_ = [
        pltpu.make_async_copy(src, dst, local_sem.at[n])
        for n, (src, dst) in enumerate((
            (w.at[half(k), :], w_buf.at[:, own_cols]),
            (code.at[quarter(k), :], c_buf.at[:, own_cols]),
            (lf.at[half(k), :], l_buf),
            (rf, r_buf.at[:, own_cols]),
            (a.at[:, half(k)], a_block(x, zh, k)),
            (g, g_block(y, zl)),
        ))
    ]
    for copy in locals_:
        copy.start()

    barrier = pltpu.get_barrier_semaphore()
    for peer in peers:
        pl.semaphore_signal(barrier, inc=1, device_id=peer, device_id_type=MESH)
    pl.semaphore_wait(barrier, len(peers))

    for j in range(2):
        for d in range(2):
            send(a.at[:, half(j)], a_block(x, zh, k), number("AX", 2 * d + j), device(x_=x_at[d], k_=j),
                 number("AX", 2 * d) + k)
    for d in range(2):
        send(g, g_block(y, zl), number("GY", 4 * d), device(y_=y_at[d]))
    for i in range(1, 4):
        send(g, g_block(y, zl), number("GZ", i - 1), device(zl_=wrap(zl + i)))
    send(rf, r_buf.at[:, sib_cols], number("R"), sibling)
    send(code.at[quarter(1 - k), :], c_buf.at[:, sib_cols], number("C"), sibling)
    send(w.at[half(1 - k), :], w_buf.at[:, sib_cols], number("W"), sibling)
    send(g, g_block(y, zl, 1), number("GS"), sibling)
    for i in range(2):
        j = k if i == 0 else 1 - k
        send(a.at[:, half(j)], a_block(x, zh, k), number("AZ", i), device(zh_=other, k_=j), number("AZ") + k)
    send(a.at[:, half(1 - k)], a_block(x, zh, k), number("AS"), sibling)

    for copy in locals_:
        copy.wait()
    merge_tiles(0, w_buf, c_buf, r_buf, l_buf, mask_buf, m_buf)

    def g_to_sibling(n, y_, zl_):
        send(g_block(y_, zl_), g_block(y_, zl_, 1), number("GS", n), sibling)

    def a_forward(name, base, zh_):
        for d in range(2):
            block = a_block(x_at[1 - d], zh_, d)
            arrived(block, number(base, 2 * d + d))
            send(block, block, number(name, d), device(x_=x_at[d]))

    def g_from_y(i):
        for d in range(2):
            from_y, from_zl = y_at[1 - d], wrap(zl + 4 - i)
            block = g_block(from_y, from_zl)
            arrived(block, number("GY", 4 * d + i))
            if i % 2 == d:
                send(block, block, number("GF", i), device(y_=y_at[d]))
            g_to_sibling(4 + 4 * d + i, from_y, from_zl)

    g_from_y(0)
    a_forward("AF", "AX", zh)
    for i in range(1, 4):
        block = g_block(y, wrap(zl + 4 - i))
        arrived(block, number("GZ", i - 1))
        for d in range(2):
            send(block, block, number("GY", 4 * d + i), device(y_=y_at[d]))
        g_to_sibling(i, y, wrap(zl + 4 - i))
    for name, ref in (("R", r_buf), ("C", c_buf), ("W", w_buf)):
        arrived(ref.at[:, sib_cols], number(name))
    merge_tiles(1, w_buf, c_buf, r_buf, l_buf, mask_buf, m_buf)
    for i in range(1, 4):
        g_from_y(i)
    for o in range(2):
        block = a_block(x, other, o)
        arrived(block, number("AZ", o))
        for d in range(2):
            send(block, block, number("AP", 2 * d + o), device(x_=x_at[d]))
    for i in range(4):
        block = g_block(wrap(y + 2), wrap(zl + 4 - i))
        arrived(block, number("GF", i))
        g_to_sibling(12 + i, wrap(y + 2), wrap(zl + 4 - i))
    arrived(g_block(y, zl, 1), number("GS"))
    for i in range(1, 4):
        arrived(g_block(y, wrap(zl + 4 - i), 1), number("GS", i))
    for d in range(2):
        for i in range(4):
            arrived(g_block(y_at[1 - d], wrap(zl + 4 - i), 1), number("GS", 4 + 4 * d + i))
    for i in range(4):
        arrived(g_block(wrap(y + 2), wrap(zl + 4 - i), 1), number("GS", 12 + i))

    def part(zh_, h):
        return pl.ds(pl.multiple_of(zh_ * 2 * TOK + h * TOK, TOK), TOK)

    zs = (other, zh)

    product(0, wrap(x + 2), g_buf, m_buf, p_buf)
    s_buf[0] = p_buf[0].astype(BF16)
    for q, zh_ in enumerate(zs):
        for d in range(2):
            send(s_buf.at[0, part(zh_, d), :], got1.at[d, zh_], number("S1", 2 * q + d), device(x_=x_at[d]),
                 number("S1", d) + 2 * zh_)
    a_forward("APF", "AP", other)
    for d in range(2):
        product(1 + d, x_at[d], g_buf, m_buf, p_buf)
        for q, zh_ in enumerate(zs):
            rows = part(zh_, 1 - d)
            s_buf[1 + d, rows, :] = p_buf[1 + d, rows, :].astype(BF16)
            send(s_buf.at[1 + d, rows, :], got2.at[d, rows, :], number("S2", 2 * q + d), device(x_=x_at[d]),
                 number("S2", d) + 2 * zh_)
    product(3, x, g_buf, m_buf, p_buf)
    for q, zh_ in enumerate(zs):
        for d in range(2):
            arrived(got1.at[d, zh_], number("S1", d) + 2 * zh_)
            rows = part(zh_, d)
            s_buf[1 + d, rows, :] = (p_buf[1 + d, rows, :] + got1[d, zh_].astype(F32)).astype(BF16)
            send(s_buf.at[1 + d, rows, :], got2.at[d, rows, :], number("S3", 2 * q + d), device(x_=x_at[d]),
                 number("S3", d) + 2 * zh_)

    arrived(a_block(x, zh, 1 - k), number("AS"))
    for d in range(2):
        arrived(a_block(x_at[1 - d], zh, 1 - d), number("AX", 2 * d + 1 - d))
        arrived(a_block(wrap(x + 2), zh, d), number("AF", d))
        arrived(a_block(x_at[1 - d], other, 1 - d), number("AP", 2 * d + 1 - d))
        arrived(a_block(wrap(x + 2), other, d), number("APF", d))
    turn(a_buf, at_buf, 0, TOKENS // TOK)
    factor_grads(at_buf, g_buf, mask_buf, r_buf, l_buf, lpart, rpart)
    for i in range(2):
        lx[x, :, i * (HALF // 2) : (i + 1) * (HALF // 2)] = lpart[i]
    for i in range(1, 4):
        send(lx.at[x], lx.at[x], number("LX", i - 1), device(x_=wrap(x + i)))
    send(rpart.at[:, sib_cols], rgot, number("RC"), sibling)

    def summed(q, zh_):
        rows = pl.ds(pl.multiple_of(zh_ * 2 * TOK, 2 * TOK), 2 * TOK)
        for d in range(2):
            arrived(got2.at[d, part(zh_, 1 - d), :], number("S2", d) + 2 * zh_)
            arrived(got2.at[d, part(zh_, d), :], number("S3", d) + 2 * zh_)
        return p_buf[3, rows, :] + got2[0, rows, :].astype(F32) + got2[1, rows, :].astype(F32)

    z_send[...] = summed(0, other).astype(BF16)
    send(z_send, z_got, number("Z"), device(zh_=other))

    arrived(rgot, number("RC"))
    ry[y] = rpart[:, :COLS] + rgot[...]
    for i in range(1, 4):
        send(ry.at[y], ry.at[y], number("RY", i - 1), device(y_=wrap(y + i)))
    for i in range(1, 4):
        arrived(lx.at[wrap(x + 4 - i)], number("LX", i - 1))
    lz[...] = (lx[0] + lx[1]) + (lx[2] + lx[3])
    for i, to in enumerate((device(zh_=other), sibling, device(zh_=other, k_=1 - k))):
        send(lz, lgot.at[i], number("LZ", i), to)
    for i in range(1, 4):
        arrived(ry.at[wrap(y + 4 - i)], number("RY", i - 1))
    rz[zl] = (ry[0] + ry[1]) + (ry[2] + ry[3])
    for i in range(1, 4):
        send(rz.at[zl], rz.at[zl], number("RZ", i - 1), device(zl_=wrap(zl + i)))
    for i in range(3):
        arrived(lgot.at[i], number("LZ", i))
    left_out[:, half(k)] = lz[...] + lgot[0]
    left_out[:, half(1 - k)] = lgot[1] + lgot[2]
    for i in range(1, 4):
        arrived(rz.at[wrap(zl + 4 - i)], number("RZ", i - 1))
    right_out[...] = (rz[0] + rz[1]) + (rz[2] + rz[3])

    p_buf[0, : 2 * TOK, :] = summed(1, zh)
    arrived(z_got, number("Z"))
    theirs = pl.ds(pl.multiple_of((1 - k) * TOK, TOK), TOK)
    ours = pl.ds(pl.multiple_of(k * TOK, TOK), TOK)
    o_send[...] = (p_buf[0, theirs, :] + z_got[theirs, :].astype(F32)).astype(BF16)
    send(o_send, out.at[:, half(k)], number("O"), sibling)
    o_own[...] = (p_buf[0, ours, :] + z_got[ours, :].astype(F32)).astype(BF16)
    last = pltpu.make_async_copy(o_own, out.at[:, half(k)], local_sem.at[0])
    last.start()
    last.wait()
    arrived(out.at[:, half(1 - k)], number("O"))
    for copy in pending:
        copy.wait_send()


def per_device(a, g, w, code, lf, rf):
    anywhere = pl.BlockSpec(memory_space=pl.ANY)
    vmem = pl.BlockSpec(memory_space=pltpu.VMEM)
    out, left, right = pl.pallas_call(
        kernel,
        out_shape=(
            jax.ShapeDtypeStruct((TOK, HID), BF16),
            jax.ShapeDtypeStruct((RANK, HID), F32),
            jax.ShapeDtypeStruct((RANK, COLS), F32),
        ),
        in_specs=[anywhere] * 6,
        out_specs=(anywhere, vmem, vmem),
        scratch_shapes=[
            pltpu.VMEM((TOKENS, HALF), BF16),
            pltpu.VMEM((HALF, TOKENS), BF16),
            pltpu.VMEM((TOKENS, BOTH), BF16),
            pltpu.VMEM((HALF, BOTH), BF16),
            pltpu.VMEM((HALF // 4, BOTH), jnp.int32),
            pltpu.VMEM((RANK, BOTH), BF16),
            pltpu.VMEM((HALF, RANK), BF16),
            pltpu.VMEM((HALF, BOTH), BF16),
            pltpu.VMEM((HALF, BOTH), BF16),
            pltpu.VMEM((4, 4 * TOK, HALF), F32),
            pltpu.VMEM((3, 4 * TOK, HALF), BF16),
            pltpu.VMEM((2, 2, TOK, HALF), BF16),
            pltpu.VMEM((2, 4 * TOK, HALF), BF16),
            pltpu.VMEM((2 * TOK, HALF), BF16),
            pltpu.VMEM((2 * TOK, HALF), BF16),
            pltpu.VMEM((TOK, HALF), BF16),
            pltpu.VMEM((TOK, HALF), BF16),
            pltpu.VMEM((2, RANK, HALF // 2), F32),
            pltpu.VMEM((4, RANK, HALF), F32),
            pltpu.VMEM((RANK, HALF), F32),
            pltpu.VMEM((3, RANK, HALF), F32),
            pltpu.VMEM((RANK, BOTH), F32),
            pltpu.VMEM((RANK, COLS), F32),
            pltpu.VMEM((4, RANK, COLS), F32),
            pltpu.VMEM((4, RANK, COLS), F32),
            pltpu.SemaphoreType.DMA((COPIES,)),
            pltpu.SemaphoreType.DMA((COPIES,)),
            pltpu.SemaphoreType.DMA((6,)),
        ],
        compiler_params=pltpu.CompilerParams(
            collective_id=0, has_side_effects=True, vmem_limit_bytes=58 << 20
        ),
        cost_estimate=pl.CostEstimate(flops=7_600_000_000, bytes_accessed=5_000_000, transcendentals=0),
        name="down_projection_backward",
    )(a, g, w, code, lf, rf)
    return out, left.T, right


def solution(mesh):
    in_specs = (
        P("col", "row"),
        P("row", "col"),
        P("row", "col"),
        P("row", "col"),
        P("row", None),
        P(None, "col"),
    )
    out_specs = (P("col", "row"), P("row", None), P(None, "col"))
    return jax.shard_map(
        per_device, mesh=mesh, in_specs=in_specs, out_specs=out_specs, check_vma=False
    )
```

time: 588 us -> 128 us (0.22)
  waiting for transfers between devices: 471 us -> 0 us
  Pallas kernels: 0 us -> 121 us
  blocking collectives: 64.2 us -> 0 us
  matrix products: 20.3 us -> 0 us
  between operations: 13.8 us -> 0.64 us
    reduce_scatter x1 -> x0, waiting for transfers between devices: 202 us -> none  [input_sums_of(): lax.psum_scatter(lax.dot_general(grad_rows, merged, (((1,), (1,)), ((), (...]
    all_gather x2 -> x0, waiting for transfers between devices: 167 us -> none  [the longest x1 97.1 us: weight_grad_of(): lax.all_gather(activations, 'col', axis=0, tiled=True)]
    pallas_call x0 -> x1, Pallas kernels: none -> 121 us  [per_device(): pl.pallas_call(kernel, out_shape=(jax.ShapeDtypeStruct((TOK, HID), BF16),...]
    psum x1 -> x0, waiting for transfers between devices: 101 us -> none  [per_device(): left_grad = lax.psum(left_partial, 'col')]
    psum x1 -> x0, blocking collectives: 64.2 us -> none  [per_device(): right_grad = lax.psum(right_partial, 'row')]
    dot_general x4 -> x0, matrix products: 20.3 us -> none  [the longest x1 9.93 us: input_sums_of(): lax.dot_general(grad_rows, merged, (((1,), (1,)), ((), ())), preferred_el...]
  transfers between devices with their start and end apart: 4 -> 0, of which waited for: 4 -> 0; matrix products, arithmetic and copies ran while one was open for 3% -> 0% of each run, Pallas kernels for 0% -> 0%
where the time goes in v1:
time: 128 us
  Pallas kernels  121 us (95%)
  local copies, waits for them, and re-layouts  6.54 us (5%)
    pallas_call x1, Pallas kernels, per_device(): pl.pallas_call(kernel, out_shape=(jax.ShapeDtypeStruct((TOK, HID), BF16),...  121 us
    unnamed x4, local copies, waits for them, and re-layouts  6.54 us

profile of v1, /device:TPU:1, one launch (start us, length us, event | category | flops | bytes accessed | tf_op | source)
XLA Modules:
  0.0 128.2 jit_solution(1708067705101173145)
XLA Ops:
  0.6 1.8 %copy.9.lf = bf16[1792,16]{1,0:T(8,128)(2,1)} copy(bf16[1792,16]{0,1:T(8,128)(2,1)} %param.10) | data formatting | bytes 114688 | tf_op args[4]
  2.4 121.0 %down_projection_backward.1 = (bf16[128,1792]{1,0:T(8,128)(2,1)}, f32[16,1792]{1,0:T(8,128)}, f32[16,512]{1,0:T(8,128)}) custom-call(bf16[128,1792]{1,0:T(8,128)(2,1)} %a.1, bf16[128,512]{1,0:T(8,128)(2,1)} %g.1, bf16[1792,512]{1,0:T(8,128)(2,1)} %w.1, s32[448,512]{1,0:T(8,128)} %code.1, bf16[1792,16]{1,0:T(8,128)(2,1)} %copy.9.lf, bf16[16,512]{1,0:T(8,128)(2,1)} %rf.1), custom_call_target="tpu_custom_call" | custom-call | flops 7600000000 | bytes 5000000 | tf_op jit(solution)/shard_map/down_projection_backward/pallas_call | solution.py:349
  123.4 1.8 %copy.13 = bf16[128,1792]{1,0:T(8,128)(2,1)} copy(bf16[128,1792]{1,0:T(8,128)(2,1)} %get-tuple-element.12) | data formatting | bytes 917504
  125.2 1.6 %copy.14 = f32[1792,16]{0,1:T(8,128)} copy(f32[1792,16]{0,1:T(8,128)} %bitcast.1) | data formatting | bytes 229376
  126.8 1.4 %copy.15 = f32[16,512]{1,0:T(8,128)} copy(f32[16,512]{1,0:T(8,128)} %get-tuple-element.14) | data formatting | bytes 65536

commit v2 on v1

v2 whole, which is shorter than its diff:
```python
import functools

import jax
import jax.numpy as jnp
from jax import lax
from jax.experimental import pallas as pl
from jax.experimental.pallas import tpu as pltpu
from jax.sharding import PartitionSpec as P

MESH = pl.DeviceIdType.MESH
BF16, F32 = jnp.bfloat16, jnp.float32
TOKENS, RANK = 2048, 16
TOK, HID, COLS = 128, 1792, 512
HALF, BOTH = HID // 2, 2 * COLS
NT = (((1,), (1,)), ((), ()))
TN = (((0,), (0,)), ((), ()))
HT = 128
PIECE = TOK // 2
WIDE = ((0, 256), (256, 256), (512, 256), (768, 128))

NUMBERS = {}


def numbered(name, count):
    NUMBERS[name] = sum(c for _, c in NUMBERS.values()), count


for _name, _count in (
    ("AX", 4), ("AZ", 2), ("AS", 1), ("AF", 2), ("AP", 4), ("APF", 2),
    ("GZ", 3), ("GY", 8), ("GF", 4), ("GS", 16),
    ("W", 1), ("C", 1), ("R", 1),
    ("S1", 8), ("S2", 8), ("S3", 8), ("Z", 2), ("O", 2),
    ("LX", 3), ("LZ", 3), ("RC", 1), ("RY", 3), ("RZ", 3),
):
    numbered(_name, _count)
COPIES = sum(c for _, c in NUMBERS.values())


def number(name, index=0):
    return NUMBERS[name][0] + index


def merge_tiles(slot, w_buf, c_buf, r_buf, l_buf, mask_buf, m_buf):
    cols = pl.ds(slot * COLS, COLS)
    groups = HT // 4
    row = lax.broadcasted_iota(jnp.int32, (HT, HT), 0)
    lane = lax.broadcasted_iota(jnp.int32, (HT, HT), 1)
    hit = (row % 4 == lane // groups) & (row // 4 == lane % groups)
    spread = jnp.where(hit, 1.0, 0.0).astype(BF16)
    right = r_buf[:, cols]

    def tile(i, _):
        code = c_buf[pl.ds(pl.multiple_of(i * groups, groups), groups), cols]
        is0, is1, is2 = code == 0, code == 1, code == 2
        is3, is4, is5 = code == 3, code == 4, code == 5
        kept = (is0 | is1 | is2, is0 | is3 | is4, is1 | is3 | is5, is2 | is4 | is5)
        kept = jnp.concatenate([jnp.where(b, 1.0, 0.0) for b in kept], axis=0).astype(BF16)
        mask = jnp.dot(spread, kept, preferred_element_type=F32)
        rows = pl.ds(pl.multiple_of(i * HT, HT), HT)
        low = lax.dot_general(l_buf[:, rows], right, TN, preferred_element_type=F32)
        merged = mask * (w_buf[rows, cols].astype(F32) + 2.0 * low)
        mask_buf[rows, cols] = mask.astype(BF16)
        m_buf[rows, cols] = merged.astype(BF16)
        return 0

    lax.fori_loop(0, HALF // HT, tile, 0)


def product(i, x_dest, g_buf, m_buf, p_buf):
    first = pl.multiple_of(x_dest * 4 * TOK, 4 * TOK)
    for at, size in WIDE:
        p_buf[i, :, at : at + size] = lax.dot_general(
            g_buf[pl.ds(first, 4 * TOK), :], m_buf[at : at + size, :], NT, preferred_element_type=F32
        )


def turn(a_buf, at_buf, first, count):
    def block(i, _):
        toks = pl.ds(pl.multiple_of(i * TOK, TOK), TOK)
        at_buf[:, toks] = a_buf[toks, :].T
        return 0

    lax.fori_loop(first, first + count, block, 0)


def factor_grads(at_buf, g_buf, mask_buf, r_buf, l_buf, left, right):
    left[...] = jnp.zeros_like(left)
    step = 256

    def tile(n, _):
        cols = pl.ds(pl.multiple_of(n * step, step), step)
        total = jnp.zeros((RANK, step), F32)
        for half in range(2):
            rows = pl.ds(half * (HALF // 2), HALF // 2)
            grad = jnp.dot(at_buf[rows, :], g_buf[:, cols], preferred_element_type=F32)
            pruned = (mask_buf[rows, cols].astype(F32) * grad * (1.0 / TOKENS)).astype(BF16)
            total += jnp.dot(l_buf[:, rows], pruned, preferred_element_type=F32)
            left[half] += 2.0 * lax.dot_general(
                r_buf[:, cols], pruned, NT, preferred_element_type=F32
            )
        right[:, cols] = 2.0 * total
        return 0

    lax.fori_loop(0, BOTH // step, tile, 0)


def kernel(
    a, g, w, code, lf, rf, out, left_out, right_out,
    a_buf, at_buf, g_buf, w_buf, c_buf, r_buf, l_buf, mask_buf, m_buf,
    p_buf, s_buf, got1, got2, z_send, z_got, o_send, o_own,
    lpart, lx, lz, lgot, rpart, rgot, ry, rz,
    send_sem, recv_sem, local_sem,
):
    row, col = lax.axis_index("row"), lax.axis_index("col")
    y, zl = row // 4, row % 4
    x, zh, k = col // 4, (col // 2) % 2, col % 2
    other = 1 - zh

    def device(y_=y, zl_=zl, x_=x, zh_=zh, k_=k):
        return (y_ * 4 + zl_, x_ * 4 + zh_ * 2 + k_)

    def wrap(v):
        return v % 4

    x_at = (wrap(x + 1), wrap(x + 3))
    y_at = (wrap(y + 1), wrap(y + 3))
    sibling = device(k_=1 - k)
    peers = [sibling]
    peers += [device(x_=x_at[d], k_=j) for d in range(2) for j in range(2)]
    peers += [device(x_=wrap(x + 2))]
    peers += [device(zh_=other, k_=j) for j in range(2)]
    peers += [device(y_=wrap(y + i)) for i in range(1, 4)]
    peers += [device(zl_=wrap(zl + i)) for i in range(1, 4)]

    pending = {}

    def send(src, dst, n, to, recv_n=None):
        copy = pltpu.make_async_remote_copy(
            src_ref=src, dst_ref=dst, send_sem=send_sem.at[n],
            recv_sem=recv_sem.at[n if recv_n is None else recv_n],
            device_id=to, device_id_type=MESH,
        )
        copy.start()
        pending[n] = copy

    def arrived(dst, n):
        pltpu.make_async_remote_copy(
            src_ref=dst, dst_ref=dst, send_sem=send_sem.at[n], recv_sem=recv_sem.at[n],
            device_id=sibling, device_id_type=MESH,
        ).wait_recv()

    def sent(n):
        pending.pop(n).wait_send()

    def tokens_of(x_, zh_, k_):
        return pl.ds(pl.multiple_of((x_ * 4 + zh_ * 2 + k_) * TOK, TOK), TOK)

    def a_block(x_, zh_, k_):
        return a_buf.at[tokens_of(x_, zh_, k_), :]

    def g_block(y_, zl_, slot=0):
        return g_buf.at[pl.ds(pl.multiple_of((y_ * 4 + zl_) * TOK, TOK), TOK), pl.ds(slot * COLS, COLS)]

    def half(j):
        return pl.ds(pl.multiple_of(j * HALF, HALF), HALF)

    def quarter(j):
        return pl.ds(pl.multiple_of(j * (HALF // 4), HALF // 4), HALF // 4)

    own_cols, sib_cols = pl.ds(0, COLS), pl.ds(COLS, COLS)

    locals_ = [
        pltpu.make_async_copy(src, dst, local_sem.at[n])
        for n, (src, dst) in enumerate((
            (w.at[half(k), :], w_buf.at[:, own_cols]),
            (code.at[quarter(k), :], c_buf.at[:, own_cols]),
            (lf.at[:, half(k)], l_buf),
            (rf, r_buf.at[:, own_cols]),
            (a.at[:, half(k)], a_block(x, zh, k)),
            (g, g_block(y, zl)),
        ))
    ]
    for copy in locals_:
        copy.start()

    barrier = pltpu.get_barrier_semaphore()
    for peer in peers:
        pl.semaphore_signal(barrier, inc=1, device_id=peer, device_id_type=MESH)
    pl.semaphore_wait(barrier, len(peers))

    def send_a_x():
        for j in range(2):
            for d in range(2):
                send(a.at[:, half(j)], a_block(x, zh, k), number("AX", 2 * d + j), device(x_=x_at[d], k_=j),
                     number("AX", 2 * d) + k)

    def send_g():
        for d in range(2):
            send(g, g_block(y, zl), number("GY", 4 * d), device(y_=y_at[d]))
        for i in (1, 3, 2):
            send(g, g_block(y, zl), number("GZ", i - 1), device(zl_=wrap(zl + i)))

    def send_a_z(i):
        j = k if i == 0 else 1 - k
        send(a.at[:, half(j)], a_block(x, zh, k), number("AZ", i), device(zh_=other, k_=j), number("AZ") + k)

    def send_sibling():
        send(g, g_block(y, zl, 1), number("GS"), sibling)
        send(rf, r_buf.at[:, sib_cols], number("R"), sibling)
        send(code.at[quarter(1 - k), :], c_buf.at[:, sib_cols], number("C"), sibling)
        send(w.at[half(1 - k), :], w_buf.at[:, sib_cols], number("W"), sibling)
        send(a.at[:, half(1 - k)], a_block(x, zh, k), number("AS"), sibling)

    def merge_own():
        for copy in locals_:
            copy.wait()
        merge_tiles(0, w_buf, c_buf, r_buf, l_buf, mask_buf, m_buf)

    def merge_sibling():
        for name, ref in (("R", r_buf), ("C", c_buf), ("W", w_buf)):
            arrived(ref.at[:, sib_cols], number(name))
        merge_tiles(1, w_buf, c_buf, r_buf, l_buf, mask_buf, m_buf)

    def g_to_sibling(n, y_, zl_):
        send(g_block(y_, zl_), g_block(y_, zl_, 1), number("GS", n), sibling)

    def a_forward(name, base, zh_, d):
        block = a_block(x_at[1 - d], zh_, d)
        arrived(block, number(base, 2 * d + d))
        send(block, block, number(name, d), device(x_=x_at[d]))

    def a_from_z(i):
        o = k if i == 0 else 1 - k
        block = a_block(x, other, o)
        arrived(block, number("AZ") + o)
        for d in range(2):
            send(block, block, number("AP", 2 * d + i), device(x_=x_at[d]), number("AP", 2 * d) + o)

    def g_from_z(i):
        block = g_block(y, wrap(zl + 4 - i))
        arrived(block, number("GZ", i - 1))
        for d in range(2):
            send(block, block, number("GY", 4 * d + i), device(y_=y_at[d]))
        g_to_sibling(i, y, wrap(zl + 4 - i))

    def g_from_y(i):
        for d in (i % 2, 1 - i % 2):
            from_y, from_zl = y_at[1 - d], wrap(zl + 4 - i)
            block = g_block(from_y, from_zl)
            arrived(block, number("GY", 4 * d + i))
            if i % 2 == d:
                send(block, block, number("GF", i), device(y_=y_at[d]))
            g_to_sibling(4 + 4 * d + i, from_y, from_zl)

    def g_from_far(i):
        block = g_block(wrap(y + 2), wrap(zl + 4 - i))
        arrived(block, number("GF", i))
        g_to_sibling(12 + i, wrap(y + 2), wrap(zl + 4 - i))

    def g_all():
        for i in range(4):
            arrived(g_block(y, wrap(zl + 4 - i), 1), number("GS", i))
        for d in range(2):
            for i in range(4):
                arrived(g_block(y_at[1 - d], wrap(zl + 4 - i), 1), number("GS", 4 + 4 * d + i))
        for i in range(4):
            arrived(g_block(wrap(y + 2), wrap(zl + 4 - i), 1), number("GS", 12 + i))

    def piece(zh_, h, u):
        return pl.ds(pl.multiple_of(zh_ * 2 * TOK + h * TOK + u * PIECE, PIECE), PIECE)

    def share_number(name, zh_, u, d):
        return number(name) + (zh_ * 4 + u * 2 + d)

    def send_far(q, u):
        zh_ = zs[q]
        for d in range(2):
            rows = piece(zh_, d, u)
            s_buf[0, rows, :] = p_buf[0, rows, :].astype(BF16)
            send(s_buf.at[0, rows, :], got1.at[d, rows, :], number("S1", 4 * q + 2 * u + d),
                 device(x_=x_at[d]), share_number("S1", zh_, u, d))

    def send_near(q, u, d):
        zh_ = zs[q]
        rows = piece(zh_, 1 - d, u)
        s_buf[1 + d, rows, :] = p_buf[1 + d, rows, :].astype(BF16)
        send(s_buf.at[1 + d, rows, :], got2.at[d, rows, :], number("S2", 4 * q + 2 * u + d),
             device(x_=x_at[d]), share_number("S2", zh_, u, d))

    def pass_on(q, u):
        zh_ = zs[q]
        for d in range(2):
            rows = piece(zh_, d, u)
            arrived(got1.at[d, rows, :], share_number("S1", zh_, u, d))
            s_buf[1 + d, rows, :] = (p_buf[1 + d, rows, :] + got1[d, rows, :].astype(F32)).astype(BF16)
            send(s_buf.at[1 + d, rows, :], got2.at[d, rows, :], number("S3", 4 * q + 2 * u + d),
                 device(x_=x_at[d]), share_number("S3", zh_, u, d))

    def summed(q, u, h):
        zh_ = zs[q]
        rows = piece(zh_, h, u)
        for d in range(2):
            arrived(got2.at[d, rows, :], share_number("S3" if h == d else "S2", zh_, u, d))
        return p_buf[3, rows, :] + got2[0, rows, :].astype(F32) + got2[1, rows, :].astype(F32)

    def send_z(u):
        for h in range(2):
            z_send[u, h * PIECE : (h + 1) * PIECE, :] = summed(0, u, h).astype(BF16)
        send(z_send.at[u], z_got.at[u], number("Z", u), device(zh_=other))

    def own_sums(u):
        for h in range(2):
            p_buf[0, h * TOK + u * PIECE : h * TOK + (u + 1) * PIECE, :] = summed(1, u, h)

    def a_rest():
        arrived(a_block(x, zh, 1 - k), number("AS"))
        for d in range(2):
            arrived(a_block(x_at[1 - d], zh, 1 - d), number("AX", 2 * d + 1 - d))
            arrived(a_block(wrap(x + 2), zh, d), number("AF", d))
            arrived(a_block(x_at[1 - d], other, 1 - d), number("AP", 2 * d + 1 - d))
            arrived(a_block(wrap(x + 2), other, d), number("APF", d))

    def factors():
        turn(a_buf, at_buf, 0, TOKENS // TOK)
        factor_grads(at_buf, g_buf, mask_buf, r_buf, l_buf, lpart, rpart)
        for i in range(2):
            lx[x, :, i * (HALF // 2) : (i + 1) * (HALF // 2)] = lpart[i]
        send(rpart.at[:, sib_cols], rgot, number("RC"), sibling)
        for i in range(1, 4):
            send(lx.at[x], lx.at[x], number("LX", i - 1), device(x_=wrap(x + i)))

    def factors_y():
        arrived(rgot, number("RC"))
        ry[y] = rpart[:, :COLS] + rgot[...]
        for i in range(1, 4):
            send(ry.at[y], ry.at[y], number("RY", i - 1), device(y_=wrap(y + i)))

    def factors_x():
        for i in range(1, 4):
            arrived(lx.at[wrap(x + 4 - i)], number("LX", i - 1))
        lz[...] = (lx[0] + lx[1]) + (lx[2] + lx[3])
        for i, to in enumerate((device(zh_=other), sibling, device(zh_=other, k_=1 - k))):
            send(lz, lgot.at[i], number("LZ", i), to)

    def factors_z():
        for i in range(1, 4):
            arrived(ry.at[wrap(y + 4 - i)], number("RY", i - 1))
        rz[zl] = (ry[0] + ry[1]) + (ry[2] + ry[3])
        for i in range(1, 4):
            send(rz.at[zl], rz.at[zl], number("RZ", i - 1), device(zl_=wrap(zl + i)))

    def factors_end():
        for i in range(3):
            arrived(lgot.at[i], number("LZ", i))
        left_out[:, half(k)] = lz[...] + lgot[0]
        left_out[:, half(1 - k)] = lgot[1] + lgot[2]
        for i in range(1, 4):
            arrived(rz.at[wrap(zl + 4 - i)], number("RZ", i - 1))
        right_out[...] = (rz[0] + rz[1]) + (rz[2] + rz[3])

    zs = (other, zh)

    send_a_x()
    send_g()
    send_sibling()
    merge_own()
    g_from_y(0)
    g_from_z(1)
    g_from_z(3)
    a_forward("AF", "AX", zh, 0)
    a_forward("AF", "AX", zh, 1)
    g_from_z(2)
    send_a_z(0)
    merge_sibling()
    g_from_y(1)
    g_from_y(3)
    g_from_far(0)
    g_from_y(2)
    g_from_far(1)
    g_from_far(3)
    g_from_far(2)
    sent(number("AZ"))
    send_a_z(1)
    a_from_z(0)
    g_all()

    product(0, wrap(x + 2), g_buf, m_buf, p_buf)
    for u in range(2):
        send_far(0, u)
    for d in range(2):
        product(1 + d, x_at[d], g_buf, m_buf, p_buf)
        for u in range(2):
            send_near(0, u, d)
    product(3, x, g_buf, m_buf, p_buf)
    a_from_z(1)
    for u in range(2):
        send_far(1, u)
    for u in range(2):
        pass_on(0, u)
    a_forward("APF", "AP", other, 0)
    a_forward("APF", "AP", other, 1)
    for u in range(2):
        for d in range(2):
            send_near(1, u, d)
    send_z(0)
    pass_on(1, 0)
    send_z(1)
    pass_on(1, 1)
    a_rest()
    factors()
    factors_y()
    factors_x()
    factors_z()
    factors_end()

    for u in range(2):
        own_sums(u)
    theirs = pl.multiple_of((1 - k) * TOK, TOK)
    ours = pl.multiple_of(k * TOK, TOK)
    for u in range(2):
        arrived(z_got.at[u], number("Z", u))
        part = slice(u * PIECE, (u + 1) * PIECE)

        def total(first, h):
            sums = p_buf[0, pl.ds(first + u * PIECE, PIECE), :]
            return (sums + z_got[u, pl.ds(pl.multiple_of(h * PIECE, PIECE), PIECE), :].astype(F32)).astype(BF16)

        o_send[part, :] = total(theirs, 1 - k)
        send(o_send.at[part, :], out.at[part, half(k)], number("O", u), sibling)
        o_own[part, :] = total(ours, k)
        pltpu.make_async_copy(o_own.at[part, :], out.at[part, half(k)], local_sem.at[u]).start()
    for u in range(2):
        part = slice(u * PIECE, (u + 1) * PIECE)
        pltpu.make_async_copy(o_own.at[part, :], out.at[part, half(k)], local_sem.at[u]).wait()
        arrived(out.at[part, half(1 - k)], number("O", u))
    for copy in pending.values():
        copy.wait_send()


def place(*arrays):
    def move(*refs):
        for src, dst in zip(refs[:3], refs[3:]):
            dst[...] = src[...]

    return pl.pallas_call(
        move,
        out_shape=tuple(jax.ShapeDtypeStruct(v.shape, v.dtype) for v in arrays),
        name="place_results",
    )(*arrays)


def per_device(a, g, w, code, lf, rf):
    anywhere = pl.BlockSpec(memory_space=pl.ANY)
    vmem = pl.BlockSpec(memory_space=pltpu.VMEM)
    out, left, right = pl.pallas_call(
        kernel,
        out_shape=(
            jax.ShapeDtypeStruct((TOK, HID), BF16),
            jax.ShapeDtypeStruct((RANK, HID), F32),
            jax.ShapeDtypeStruct((RANK, COLS), F32),
        ),
        in_specs=[anywhere] * 6,
        out_specs=(anywhere, vmem, vmem),
        scratch_shapes=[
            pltpu.VMEM((TOKENS, HALF), BF16),
            pltpu.VMEM((HALF, TOKENS), BF16),
            pltpu.VMEM((TOKENS, BOTH), BF16),
            pltpu.VMEM((HALF, BOTH), BF16),
            pltpu.VMEM((HALF // 4, BOTH), jnp.int32),
            pltpu.VMEM((RANK, BOTH), BF16),
            pltpu.VMEM((RANK, HALF), BF16),
            pltpu.VMEM((HALF, BOTH), BF16),
            pltpu.VMEM((HALF, BOTH), BF16),
            pltpu.VMEM((4, 4 * TOK, HALF), F32),
            pltpu.VMEM((3, 4 * TOK, HALF), BF16),
            pltpu.VMEM((2, 4 * TOK, HALF), BF16),
            pltpu.VMEM((2, 4 * TOK, HALF), BF16),
            pltpu.VMEM((2, TOK, HALF), BF16),
            pltpu.VMEM((2, TOK, HALF), BF16),
            pltpu.VMEM((TOK, HALF), BF16),
            pltpu.VMEM((TOK, HALF), BF16),
            pltpu.VMEM((2, RANK, HALF // 2), F32),
            pltpu.VMEM((4, RANK, HALF), F32),
            pltpu.VMEM((RANK, HALF), F32),
            pltpu.VMEM((3, RANK, HALF), F32),
            pltpu.VMEM((RANK, BOTH), F32),
            pltpu.VMEM((RANK, COLS), F32),
            pltpu.VMEM((4, RANK, COLS), F32),
            pltpu.VMEM((4, RANK, COLS), F32),
            pltpu.SemaphoreType.DMA((COPIES,)),
            pltpu.SemaphoreType.DMA((COPIES,)),
            pltpu.SemaphoreType.DMA((6,)),
        ],
        compiler_params=pltpu.CompilerParams(
            collective_id=0, has_side_effects=True, vmem_limit_bytes=58 << 20
        ),
        cost_estimate=pl.CostEstimate(flops=7_600_000_000, bytes_accessed=5_000_000, transcendentals=0),
        name="down_projection_backward",
    )(a, g, w, code, lf.T, rf)
    out, left, right = place(out, left, right)
    return out, left.T, right


def solution(mesh):
    in_specs = (
        P("col", "row"),
        P("row", "col"),
        P("row", "col"),
        P("row", "col"),
        P("row", None),
        P(None, "col"),
    )
    out_specs = (P("col", "row"), P("row", None), P(None, "col"))
    return jax.shard_map(
        per_device, mesh=mesh, in_specs=in_specs, out_specs=out_specs, check_vma=False
    )
```

time: 128 us -> 104 us (0.81)
  Pallas kernels: 121 us -> 103 us
  local copies, waits for them, and re-layouts: 6.54 us -> 0 us
    pallas_call x1, Pallas kernels: 121 us -> 101 us  [per_device(): pl.pallas_call(kernel, out_shape=(jax.ShapeDtypeStruct((TOK, HID), BF16),...]
    unnamed x4 -> x0, local copies, waits for them, and re-layouts: 6.54 us -> none
    pallas_call x0 -> x1, Pallas kernels: none -> 1.9 us  [place(): pl.pallas_call(move, out_shape=tuple((jax.ShapeDtypeStruct(v.shape, v.dty...]
where the time goes in v2:
time: 104 us
  Pallas kernels  103 us (99%)
    pallas_call x1, Pallas kernels, per_device(): pl.pallas_call(kernel, out_shape=(jax.ShapeDtypeStruct((TOK, HID), BF16),...  101 us

profile of v2, /device:TPU:1, one launch (start us, length us, event | category | flops | bytes accessed | tf_op | source)
XLA Modules:
  0.0 103.5 jit_solution(3946490203729983939)
XLA Ops:
  0.6 101.0 %down_projection_backward.1 = (bf16[128,1792]{1,0:T(8,128)(2,1)}, f32[16,1792]{1,0:T(8,128)}, f32[16,512]{1,0:T(8,128)}) custom-call(bf16[128,1792]{1,0:T(8,128)(2,1)} %a.1, bf16[128,512]{1,0:T(8,128)(2,1)} %g.1, bf16[1792,512]{1,0:T(8,128)(2,1)} %w.1, s32[448,512]{1,0:T(8,128)} %code.1, bf16[16,1792]{1,0:T(8,128)(2,1)} %bitcast.3, bf16[16,512]{1,0:T(8,128)(2,1)} %rf.1), custom_call_target="tpu_custom_call" | custom-call | flops 7600000000 | bytes 5000000 | tf_op jit(solution)/shard_map/down_projection_backward/pallas_call | solution.py:455
  101.6 1.9 %place_results.1 = (bf16[128,1792]{1,0:T(8,128)(2,1)}, f32[16,1792]{1,0:T(8,128)}, f32[16,512]{1,0:T(8,128)}) custom-call(bf16[128,1792]{1,0:T(8,128)(2,1)} %get-tuple-element.9.refs_0_, f32[16,1792]{1,0:T(8,128)} %get-tuple-element.10.refs_1_, f32[16,512]{1,0:T(8,128)} %get-tuple-element.11.refs_2_), custom_call_target="tpu_custom_call" | custom-call | tf_op jit(solution)/shard_map/place_results/pallas_call | solution.py:445

commit v3 on v2

--- a/solution.py
+++ b/solution.py
@@ -16,6 +16,7 @@
 TN = (((0,), (0,)), ((), ()))
 HT = 128
 PIECE = TOK // 2
+LROWS, RCOLS = RANK // 4, COLS // 4
 WIDE = ((0, 256), (256, 256), (512, 256), (768, 128))
 
 NUMBERS = {}
@@ -30,7 +31,7 @@
     ("GZ", 3), ("GY", 8), ("GF", 4), ("GS", 16),
     ("W", 1), ("C", 1), ("R", 1),
     ("S1", 8), ("S2", 8), ("S3", 8), ("Z", 2), ("O", 2),
-    ("LX", 3), ("LZ", 3), ("RC", 1), ("RY", 3), ("RZ", 3),
+    ("LX", 3), ("LZ", 1), ("LG", 7), ("RC", 1), ("RY", 3), ("RZ", 3), ("RG", 3),
 ):
     numbered(_name, _count)
 COPIES = sum(c for _, c in NUMBERS.values())
@@ -74,18 +75,19 @@
         )
 
 
-def turn(a_buf, at_buf, first, count):
+def turn(a_buf, at_buf, zh):
     def block(i, _):
-        toks = pl.ds(pl.multiple_of(i * TOK, TOK), TOK)
+        toks = pl.ds(pl.multiple_of(((i // 2) * 4 + zh * 2 + i % 2) * TOK, TOK), TOK)
         at_buf[:, toks] = a_buf[toks, :].T
         return 0
 
-    lax.fori_loop(first, first + count, block, 0)
-
-
-def factor_grads(at_buf, g_buf, mask_buf, r_buf, l_buf, left, right):
-    left[...] = jnp.zeros_like(left)
-    step = 256
+    lax.fori_loop(0, TOKENS // TOK // 2, block, 0)
+
+
+def factor_grads(first, last, at_buf, g_buf, mask_buf, r_buf, l_buf, left, right):
+    if first == 0:
+        left[...] = jnp.zeros_like(left)
+    step = 512
 
     def tile(n, _):
         cols = pl.ds(pl.multiple_of(n * step, step), step)
@@ -101,14 +103,14 @@
         right[:, cols] = 2.0 * total
         return 0
 
-    lax.fori_loop(0, BOTH // step, tile, 0)
+    lax.fori_loop(first, last, tile, 0)
 
 
 def kernel(
     a, g, w, code, lf, rf, out, left_out, right_out,
     a_buf, at_buf, g_buf, w_buf, c_buf, r_buf, l_buf, mask_buf, m_buf,
     p_buf, s_buf, got1, got2, z_send, z_got, o_send, o_own,
-    lpart, lx, lz, lgot, rpart, rgot, ry, rz,
+    lpart, lx_send, lx, lz, lz_got, lall, rpart, rgot, ry_send, ry, rz, rall,
     send_sem, recv_sem, local_sem,
 ):
     row, col = lax.axis_index("row"), lax.axis_index("col")
@@ -127,27 +129,34 @@
     sibling = device(k_=1 - k)
     peers = [sibling]
     peers += [device(x_=x_at[d], k_=j) for d in range(2) for j in range(2)]
-    peers += [device(x_=wrap(x + 2))]
+    peers += [device(x_=wrap(x + 2), k_=j) for j in range(2)]
     peers += [device(zh_=other, k_=j) for j in range(2)]
     peers += [device(y_=wrap(y + i)) for i in range(1, 4)]
     peers += [device(zl_=wrap(zl + i)) for i in range(1, 4)]
 
     pending = {}
 
-    def send(src, dst, n, to, recv_n=None):
+    def send(src, dst, n, to, recv_n=None, keep=True):
         copy = pltpu.make_async_remote_copy(
             src_ref=src, dst_ref=dst, send_sem=send_sem.at[n],
             recv_sem=recv_sem.at[n if recv_n is None else recv_n],
             device_id=to, device_id_type=MESH,
         )
         copy.start()
-        pending[n] = copy
+        if keep:
+            pending[n] = copy
 
     def arrived(dst, n):
         pltpu.make_async_remote_copy(
             src_ref=dst, dst_ref=dst, send_sem=send_sem.at[n], recv_sem=recv_sem.at[n],
             device_id=sibling, device_id_type=MESH,
         ).wait_recv()
+
+    def left(src, n):
+        pltpu.make_async_remote_copy(
+            src_ref=src, dst_ref=src, send_sem=send_sem.at[n], recv_sem=recv_sem.at[n],
+            device_id=sibling, device_id_type=MESH,
+        ).wait_send()
 
     def sent(n):
         pending.pop(n).wait_send()
@@ -257,14 +266,10 @@
         arrived(block, number("GF", i))
         g_to_sibling(12 + i, wrap(y + 2), wrap(zl + 4 - i))
 
-    def g_all():
+    def g_row(e):
+        first = {0: 0, 3: 4, 1: 8, 2: 12}[e]
         for i in range(4):
-            arrived(g_block(y, wrap(zl + 4 - i), 1), number("GS", i))
-        for d in range(2):
-            for i in range(4):
-                arrived(g_block(y_at[1 - d], wrap(zl + 4 - i), 1), number("GS", 4 + 4 * d + i))
-        for i in range(4):
-            arrived(g_block(wrap(y + 2), wrap(zl + 4 - i), 1), number("GS", 12 + i))
+            arrived(g_block(wrap(y + e), wrap(zl + 4 - i), 1), number("GS", first + i))
 
     def piece(zh_, h, u):
         return pl.ds(pl.multiple_of(zh_ * 2 * TOK + h * TOK + u * PIECE, PIECE), PIECE)
@@ -276,24 +281,61 @@
         zh_ = zs[q]
         for d in range(2):
             rows = piece(zh_, d, u)
-            s_buf[0, rows, :] = p_buf[0, rows, :].astype(BF16)
-            send(s_buf.at[0, rows, :], got1.at[d, rows, :], number("S1", 4 * q + 2 * u + d),
-                 device(x_=x_at[d]), share_number("S1", zh_, u, d))
+            s_buf[2, rows, :] = p_buf[2, rows, :].astype(BF16)
+            send(s_buf.at[2, rows, :], got1.at[d, rows, :], number("S1", 4 * q + 2 * u + d),
+                 device(x_=x_at[d]), share_number("S1", zh_, u, d), keep=False)
 
     def send_near(q, u, d):
         zh_ = zs[q]
         rows = piece(zh_, 1 - d, u)
-        s_buf[1 + d, rows, :] = p_buf[1 + d, rows, :].astype(BF16)
-        send(s_buf.at[1 + d, rows, :], got2.at[d, rows, :], number("S2", 4 * q + 2 * u + d),
-             device(x_=x_at[d]), share_number("S2", zh_, u, d))
+        to = 1 + 2 * d
+        s_buf[to, rows, :] = p_buf[to, rows, :].astype(BF16)
+        send(s_buf.at[to, rows, :], got2.at[d, rows, :], number("S2", 4 * q + 2 * u + d),
+             device(x_=x_at[d]), share_number("S2", zh_, u, d), keep=False)
+
+    def shares(e):
+        g_row(e)
+        place_ = wrap(y + e + 4 - x)
+        product(place_, wrap(y + e), g_buf, m_buf, p_buf)
+        early = (0, 1) if e == 0 else (0,)
+
+        @pl.when(place_ == 2)
+        def _():
+            for q in early:
+                for u in range(2):
+                    send_far(q, u)
+
+        for d in range(2):
+
+            @pl.when(place_ == 1 + 2 * d)
+            def _():
+                for q in early:
+                    for u in range(2):
+                        send_near(q, u, d)
+
+    def shares_later():
+        place_ = wrap(y + 4 - x)
+
+        @pl.when(place_ != 2)
+        def _():
+            for u in range(2):
+                send_far(1, u)
+
+        for d in range(2):
+
+            @pl.when(place_ != 1 + 2 * d)
+            def _():
+                for u in range(2):
+                    send_near(1, u, d)
 
     def pass_on(q, u):
         zh_ = zs[q]
         for d in range(2):
             rows = piece(zh_, d, u)
             arrived(got1.at[d, rows, :], share_number("S1", zh_, u, d))
-            s_buf[1 + d, rows, :] = (p_buf[1 + d, rows, :] + got1[d, rows, :].astype(F32)).astype(BF16)
-            send(s_buf.at[1 + d, rows, :], got2.at[d, rows, :], number("S3", 4 * q + 2 * u + d),
+            to = 1 + 2 * d
+            s_buf[to, rows, :] = (p_buf[to, rows, :] + got1[d, rows, :].astype(F32)).astype(BF16)
+            send(s_buf.at[to, rows, :], got2.at[d, rows, :], number("S3", 4 * q + 2 * u + d),
                  device(x_=x_at[d]), share_number("S3", zh_, u, d))
 
     def summed(q, u, h):
@@ -301,7 +343,7 @@
         rows = piece(zh_, h, u)
         for d in range(2):
             arrived(got2.at[d, rows, :], share_number("S3" if h == d else "S2", zh_, u, d))
-        return p_buf[3, rows, :] + got2[0, rows, :].astype(F32) + got2[1, rows, :].astype(F32)
+        return p_buf[0, rows, :] + got2[0, rows, :].astype(F32) + got2[1, rows, :].astype(F32)
 
     def send_z(u):
         for h in range(2):
@@ -310,37 +352,40 @@
 
     def own_sums(u):
         for h in range(2):
-            p_buf[0, h * TOK + u * PIECE : h * TOK + (u + 1) * PIECE, :] = summed(1, u, h)
-
-    def a_rest():
-        arrived(a_block(x, zh, 1 - k), number("AS"))
-        for d in range(2):
-            arrived(a_block(x_at[1 - d], zh, 1 - d), number("AX", 2 * d + 1 - d))
-            arrived(a_block(wrap(x + 2), zh, d), number("AF", d))
-            arrived(a_block(x_at[1 - d], other, 1 - d), number("AP", 2 * d + 1 - d))
-            arrived(a_block(wrap(x + 2), other, d), number("APF", d))
-
-    def factors():
-        turn(a_buf, at_buf, 0, TOKENS // TOK)
-        factor_grads(at_buf, g_buf, mask_buf, r_buf, l_buf, lpart, rpart)
-        for i in range(2):
-            lx[x, :, i * (HALF // 2) : (i + 1) * (HALF // 2)] = lpart[i]
+            p_buf[2, h * TOK + u * PIECE : h * TOK + (u + 1) * PIECE, :] = summed(1, u, h)
+
+    def a_rest(zh_, near, far):
+        for d in range(2):
+            arrived(a_block(x_at[1 - d], zh_, 1 - d), number(near, 2 * d + 1 - d))
+            arrived(a_block(wrap(x + 2), zh_, d), number(far, d))
+        turn(a_buf, at_buf, zh_)
+
+    def factors(first, last):
+        factor_grads(first, last, at_buf, g_buf, mask_buf, r_buf, l_buf, lpart, rpart)
+
+    def factors_send():
         send(rpart.at[:, sib_cols], rgot, number("RC"), sibling)
-        for i in range(1, 4):
-            send(lx.at[x], lx.at[x], number("LX", i - 1), device(x_=wrap(x + i)))
+        for q in range(4):
+            rows = slice(q * LROWS, (q + 1) * LROWS)
+            lx_send[q] = jnp.concatenate([lpart[0, rows, :], lpart[1, rows, :]], axis=1)
+        lx[x] = lx_send[x]
+        for i in range(1, 4):
+            send(lx_send.at[wrap(x + i)], lx.at[x], number("LX", i - 1), device(x_=wrap(x + i)))
 
     def factors_y():
         arrived(rgot, number("RC"))
-        ry[y] = rpart[:, :COLS] + rgot[...]
-        for i in range(1, 4):
-            send(ry.at[y], ry.at[y], number("RY", i - 1), device(y_=wrap(y + i)))
+        for q in range(4):
+            lanes = slice(q * RCOLS, (q + 1) * RCOLS)
+            ry_send[q] = rpart[:, lanes] + rgot[:, lanes]
+        ry[y] = ry_send[y]
+        for i in range(1, 4):
+            send(ry_send.at[wrap(y + i)], ry.at[y], number("RY", i - 1), device(y_=wrap(y + i)))
 
     def factors_x():
         for i in range(1, 4):
             arrived(lx.at[wrap(x + 4 - i)], number("LX", i - 1))
         lz[...] = (lx[0] + lx[1]) + (lx[2] + lx[3])
-        for i, to in enumerate((device(zh_=other), sibling, device(zh_=other, k_=1 - k))):
-            send(lz, lgot.at[i], number("LZ", i), to)
+        send(lz, lz_got, number("LZ"), device(zh_=other))
 
     def factors_z():
         for i in range(1, 4):
@@ -349,14 +394,34 @@
         for i in range(1, 4):
             send(rz.at[zl], rz.at[zl], number("RZ", i - 1), device(zl_=wrap(zl + i)))
 
+    def left_share():
+        arrived(lz_got, number("LZ"))
+        lall[k, x] = lz[...] + lz_got[...]
+        for i in range(4):
+            for c in range(2):
+                if i or c:
+                    send(lall.at[k, x], lall.at[k, x], number("LG", 2 * i + c - 1),
+                         device(x_=wrap(x + i), k_=k if c == 0 else 1 - k))
+
+    def right_share():
+        for i in range(1, 4):
+            arrived(rz.at[wrap(zl + 4 - i)], number("RZ", i - 1))
+        rall[y] = (rz[0] + rz[1]) + (rz[2] + rz[3])
+        for i in range(1, 4):
+            send(rall.at[y], rall.at[y], number("RG", i - 1), device(y_=wrap(y + i)))
+
     def factors_end():
-        for i in range(3):
-            arrived(lgot.at[i], number("LZ", i))
-        left_out[:, half(k)] = lz[...] + lgot[0]
-        left_out[:, half(1 - k)] = lgot[1] + lgot[2]
-        for i in range(1, 4):
-            arrived(rz.at[wrap(zl + 4 - i)], number("RZ", i - 1))
-        right_out[...] = (rz[0] + rz[1]) + (rz[2] + rz[3])
+        for i in range(4):
+            for c in range(2):
+                if i or c:
+                    arrived(lall.at[k if c == 0 else 1 - k, wrap(x + 4 - i)], number("LG", 2 * i + c - 1))
+        for c in range(2):
+            for q in range(4):
+                left_out[q * LROWS : (q + 1) * LROWS, c * HALF : (c + 1) * HALF] = lall[c, q]
+        for i in range(1, 4):
+            arrived(rall.at[wrap(y + 4 - i)], number("RG", i - 1))
+        for q in range(4):
+            right_out[:, q * RCOLS : (q + 1) * RCOLS] = rall[q]
 
     zs = (other, zh)
 
@@ -372,49 +437,45 @@
     g_from_z(2)
     send_a_z(0)
     merge_sibling()
+    shares(0)
     g_from_y(1)
     g_from_y(3)
     g_from_far(0)
     g_from_y(2)
     g_from_far(1)
+    shares(3)
+    shares(1)
     g_from_far(3)
     g_from_far(2)
     sent(number("AZ"))
     send_a_z(1)
     a_from_z(0)
-    g_all()
-
-    product(0, wrap(x + 2), g_buf, m_buf, p_buf)
-    for u in range(2):
-        send_far(0, u)
-    for d in range(2):
-        product(1 + d, x_at[d], g_buf, m_buf, p_buf)
-        for u in range(2):
-            send_near(0, u, d)
-    product(3, x, g_buf, m_buf, p_buf)
+    shares(2)
+    arrived(a_block(x, zh, 1 - k), number("AS"))
+    a_rest(zh, "AX", "AF")
     a_from_z(1)
-    for u in range(2):
-        send_far(1, u)
-    for u in range(2):
-        pass_on(0, u)
+    pass_on(0, 0)
+    pass_on(0, 1)
     a_forward("APF", "AP", other, 0)
     a_forward("APF", "AP", other, 1)
-    for u in range(2):
-        for d in range(2):
-            send_near(1, u, d)
     send_z(0)
+    shares_later()
+    send_z(1)
+    a_rest(other, "AP", "APF")
+    factors(0, 1)
     pass_on(1, 0)
-    send_z(1)
     pass_on(1, 1)
-    a_rest()
-    factors()
+    factors(1, 2)
+    factors_send()
     factors_y()
     factors_x()
     factors_z()
-    factors_end()
+    left_share()
+    right_share()
 
     for u in range(2):
         own_sums(u)
+    factors_end()
     theirs = pl.multiple_of((1 - k) * TOK, TOK)
     ours = pl.multiple_of(k * TOK, TOK)
     for u in range(2):
@@ -422,7 +483,7 @@
         part = slice(u * PIECE, (u + 1) * PIECE)
 
         def total(first, h):
-            sums = p_buf[0, pl.ds(first + u * PIECE, PIECE), :]
+            sums = p_buf[2, pl.ds(first + u * PIECE, PIECE), :]
             return (sums + z_got[u, pl.ds(pl.multiple_of(h * PIECE, PIECE), PIECE), :].astype(F32)).astype(BF16)
 
         o_send[part, :] = total(theirs, 1 - k)
@@ -435,6 +496,9 @@
         arrived(out.at[part, half(1 - k)], number("O", u))
     for copy in pending.values():
         copy.wait_send()
+    for n in range(8):
+        for name in ("S1", "S2"):
+            left(s_buf.at[0, pl.ds(0, PIECE), :], number(name, n))
 
 
 def place(*arrays):
@@ -472,7 +536,7 @@
             pltpu.VMEM((HALF, BOTH), BF16),
             pltpu.VMEM((HALF, BOTH), BF16),
             pltpu.VMEM((4, 4 * TOK, HALF), F32),
-            pltpu.VMEM((3, 4 * TOK, HALF), BF16),
+            pltpu.VMEM((4, 4 * TOK, HALF), BF16),
             pltpu.VMEM((2, 4 * TOK, HALF), BF16),
             pltpu.VMEM((2, 4 * TOK, HALF), BF16),
             pltpu.VMEM((2, TOK, HALF), BF16),
@@ -480,13 +544,17 @@
             pltpu.VMEM((TOK, HALF), BF16),
             pltpu.VMEM((TOK, HALF), BF16),
             pltpu.VMEM((2, RANK, HALF // 2), F32),
-            pltpu.VMEM((4, RANK, HALF), F32),
-            pltpu.VMEM((RANK, HALF), F32),
-            pltpu.VMEM((3, RANK, HALF), F32),
+            pltpu.VMEM((4, LROWS, HALF), F32),
+            pltpu.VMEM((4, LROWS, HALF), F32),
+            pltpu.VMEM((LROWS, HALF), F32),
+            pltpu.VMEM((LROWS, HALF), F32),
+            pltpu.VMEM((2, 4, LROWS, HALF), F32),
             pltpu.VMEM((RANK, BOTH), F32),
             pltpu.VMEM((RANK, COLS), F32),
-            pltpu.VMEM((4, RANK, COLS), F32),
-            pltpu.VMEM((4, RANK, COLS), F32),
+            pltpu.VMEM((4, RANK, RCOLS), F32),
+            pltpu.VMEM((4, RANK, RCOLS), F32),
+            pltpu.VMEM((4, RANK, RCOLS), F32),
+            pltpu.VMEM((4, RANK, RCOLS), F32),
             pltpu.SemaphoreType.DMA((COPIES,)),
             pltpu.SemaphoreType.DMA((COPIES,)),
             pltpu.SemaphoreType.DMA((6,)),

time: 104 us -> 96.4 us (0.927)
  Pallas kernels: 103 us -> 95.6 us
    pallas_call x1, Pallas kernels: 101 us -> 93.7 us  [per_device(): pl.pallas_call(kernel, out_shape=(jax.ShapeDtypeStruct((TOK, HID), BF16),...]
where the time goes in v3:
time: 96.4 us; the launch traced here: 96.3 us
  Pallas kernels  95.6 us (99%)
    pallas_call x1, Pallas kernels, per_device(): pl.pallas_call(kernel, out_shape=(jax.ShapeDtypeStruct((TOK, HID), BF16),...  93.7 us

profile of v3, /device:TPU:1, one launch (start us, length us, event | category | flops | bytes accessed | tf_op | source)
XLA Modules:
  0.0 96.3 jit_solution(16426504371613033632)
XLA Ops:
  0.6 93.7 %down_projection_backward.1 = (bf16[128,1792]{1,0:T(8,128)(2,1)}, f32[16,1792]{1,0:T(8,128)}, f32[16,512]{1,0:T(8,128)}) custom-call(bf16[128,1792]{1,0:T(8,128)(2,1)} %a.1, bf16[128,512]{1,0:T(8,128)(2,1)} %g.1, bf16[1792,512]{1,0:T(8,128)(2,1)} %w.1, s32[448,512]{1,0:T(8,128)} %code.1, bf16[16,1792]{1,0:T(8,128)(2,1)} %bitcast.3, bf16[16,512]{1,0:T(8,128)(2,1)} %rf.1), custom_call_target="tpu_custom_call" | custom-call | flops 7600000000 | bytes 5000000 | tf_op jit(solution)/shard_map/down_projection_backward/pallas_call | solution.py:519
  94.4 1.9 %place_results.1 = (bf16[128,1792]{1,0:T(8,128)(2,1)}, f32[16,1792]{1,0:T(8,128)}, f32[16,512]{1,0:T(8,128)}) custom-call(bf16[128,1792]{1,0:T(8,128)(2,1)} %get-tuple-element.9.refs_0_, f32[16,1792]{1,0:T(8,128)} %get-tuple-element.10.refs_1_, f32[16,512]{1,0:T(8,128)} %get-tuple-element.11.refs_2_), custom_call_target="tpu_custom_call" | custom-call | tf_op jit(solution)/shard_map/place_results/pallas_call | solution.py:509

commit v4 on v3

--- a/solution.py
+++ b/solution.py
@@ -462,20 +462,18 @@
     shares_later()
     send_z(1)
     a_rest(other, "AP", "APF")
-    factors(0, 1)
+    factors(0, 2)
+    factors_send()
     pass_on(1, 0)
+    factors_y()
     pass_on(1, 1)
-    factors(1, 2)
-    factors_send()
-    factors_y()
     factors_x()
     factors_z()
+
+    own_sums(0)
     left_share()
     right_share()
-
-    for u in range(2):
-        own_sums(u)
-    factors_end()
+    own_sums(1)
     theirs = pl.multiple_of((1 - k) * TOK, TOK)
     ours = pl.multiple_of(k * TOK, TOK)
     for u in range(2):
@@ -490,6 +488,7 @@
         send(o_send.at[part, :], out.at[part, half(k)], number("O", u), sibling)
         o_own[part, :] = total(ours, k)
         pltpu.make_async_copy(o_own.at[part, :], out.at[part, half(k)], local_sem.at[u]).start()
+    factors_end()
     for u in range(2):
         part = slice(u * PIECE, (u + 1) * PIECE)
         pltpu.make_async_copy(o_own.at[part, :], out.at[part, half(k)], local_sem.at[u]).wait()

time: 96.4 us -> 91.9 us (0.953)
  Pallas kernels: 95.6 us -> 91.1 us
    pallas_call x1, Pallas kernels: 93.7 us -> 89.2 us  [per_device(): pl.pallas_call(kernel, out_shape=(jax.ShapeDtypeStruct((TOK, HID), BF16),...]
where the time goes in v4:
time: 91.9 us; the launch traced here: 91.8 us
  Pallas kernels  91.1 us (99%)
    pallas_call x1, Pallas kernels, per_device(): pl.pallas_call(kernel, out_shape=(jax.ShapeDtypeStruct((TOK, HID), BF16),...  89.2 us
    pallas_call x1, Pallas kernels, place(): pl.pallas_call(move, out_shape=tuple((jax.ShapeDtypeStruct(v.shape, v.dty...  1.9 us

profile of v4, /device:TPU:1, one launch (start us, length us, event | category | flops | bytes accessed | tf_op | source)
XLA Modules:
  0.0 91.8 jit_solution(10139942689333104037)
XLA Ops:
  0.6 89.2 %down_projection_backward.1 = (bf16[128,1792]{1,0:T(8,128)(2,1)}, f32[16,1792]{1,0:T(8,128)}, f32[16,512]{1,0:T(8,128)}) custom-call(bf16[128,1792]{1,0:T(8,128)(2,1)} %a.1, bf16[128,512]{1,0:T(8,128)(2,1)} %g.1, bf16[1792,512]{1,0:T(8,128)(2,1)} %w.1, s32[448,512]{1,0:T(8,128)} %code.1, bf16[16,1792]{1,0:T(8,128)(2,1)} %bitcast.3, bf16[16,512]{1,0:T(8,128)(2,1)} %rf.1), custom_call_target="tpu_custom_call" | custom-call | flops 7600000000 | bytes 5000000 | tf_op jit(solution)/shard_map/down_projection_backward/pallas_call | solution.py:518
  89.9 1.9 %place_results.1 = (bf16[128,1792]{1,0:T(8,128)(2,1)}, f32[16,1792]{1,0:T(8,128)}, f32[16,512]{1,0:T(8,128)}) custom-call(bf16[128,1792]{1,0:T(8,128)(2,1)} %get-tuple-element.9.refs_0_, f32[16,1792]{1,0:T(8,128)} %get-tuple-element.10.refs_1_, f32[16,512]{1,0:T(8,128)} %get-tuple-element.11.refs_2_), custom_call_target="tpu_custom_call" | custom-call | tf_op jit(solution)/shard_map/place_results/pallas_call | solution.py:508

commit v5 on v4

--- a/solution.py
+++ b/solution.py
@@ -470,8 +470,8 @@
     factors_x()
     factors_z()
 
+    left_share()
     own_sums(0)
-    left_share()
     right_share()
     own_sums(1)
     theirs = pl.multiple_of((1 - k) * TOK, TOK)

time: 91.9 us -> 91.9 us (level)
  no operation moved by 1% of the time
where the time goes in v5:
time: 91.9 us; the launch traced here: 91.8 us
  Pallas kernels  91.1 us (99%)
    pallas_call x1, Pallas kernels, per_device(): pl.pallas_call(kernel, out_shape=(jax.ShapeDtypeStruct((TOK, HID), BF16),...  89.2 us
    pallas_call x1, Pallas kernels, place(): pl.pallas_call(move, out_shape=tuple((jax.ShapeDtypeStruct(v.shape, v.dty...  1.9 us

profile of v5, /device:TPU:1, one launch (start us, length us, event | category | flops | bytes accessed | tf_op | source)
XLA Modules:
  0.0 91.8 jit_solution(13611569023525834169)
XLA Ops:
  0.6 89.2 %down_projection_backward.1 = (bf16[128,1792]{1,0:T(8,128)(2,1)}, f32[16,1792]{1,0:T(8,128)}, f32[16,512]{1,0:T(8,128)}) custom-call(bf16[128,1792]{1,0:T(8,128)(2,1)} %a.1, bf16[128,512]{1,0:T(8,128)(2,1)} %g.1, bf16[1792,512]{1,0:T(8,128)(2,1)} %w.1, s32[448,512]{1,0:T(8,128)} %code.1, bf16[16,1792]{1,0:T(8,128)(2,1)} %bitcast.3, bf16[16,512]{1,0:T(8,128)(2,1)} %rf.1), custom_call_target="tpu_custom_call" | custom-call | flops 7600000000 | bytes 5000000 | tf_op jit(solution)/shard_map/down_projection_backward/pallas_call | solution.py:518
  89.9 1.9 %place_results.1 = (bf16[128,1792]{1,0:T(8,128)(2,1)}, f32[16,1792]{1,0:T(8,128)}, f32[16,512]{1,0:T(8,128)}) custom-call(bf16[128,1792]{1,0:T(8,128)(2,1)} %get-tuple-element.9.refs_0_, f32[16,1792]{1,0:T(8,128)} %get-tuple-element.10.refs_1_, f32[16,512]{1,0:T(8,128)} %get-tuple-element.11.refs_2_), custom_call_target="tpu_custom_call" | custom-call | tf_op jit(solution)/shard_map/place_results/pallas_call | solution.py:508
